TPU v7x, 512 devices: a whole 4x8x8 slice. The times are simulated.
512 devices in a mesh: inst: 32 (over x, z), head: 16 (over y, core).
Axes of the slice: x: 4, y: 8, z: 8, core: 2. Of those that a mesh axis runs over, the one named last changes fastest.
Arguments:
- hidden_rows: bfloat16 [32, 32, 16, 9216], P('inst', None, None, 'head'), may hold values from -6 to 6
- send_counts: int32 [32, 32], P('inst'), may hold values from 0 to 16, as said below
- row_session: int32 [32, 32, 16], P('inst'), may hold values from 0 to 1, as said below
- row_position: int32 [32, 32, 16], P('inst'), may hold values from 0 to 1023, as said below
- resident_lengths: int32 [64], P('inst'), may hold values from 1 to 512, as said below
- kv_weight: bfloat16 [9216, 12288], P('inst', 'head'), may hold values from -0.0625 to 0.0625
- key_cache: bfloat16 [64, 1024, 6144], P('inst', None, 'head'), as said below
- value_cache: bfloat16 [64, 1024, 6144], P('inst', None, 'head'), may hold values from -6 to 6
- query: bfloat16 [64, 6144], P('inst', 'head'), as said below
- new_key: bfloat16 [64, 6144], P('inst', 'head'), may hold values from -6 to 6
- new_value: bfloat16 [64, 6144], P('inst', 'head'), may hold values from -6 to 6
Outputs:
- attended: bfloat16 [64, 6144], P('inst', 'head')
Inputs may be any that keep to these rules, and one draw needn't show every extreme that they name: `send_counts`: at most 16 live slots from one source to one destination; in every draw one destination instance receives 16 rows from every source. `row_session`: for a live slot, a session of the destination instance; 0 in slots that are not live. The destination that receives 16 rows from every source sends all of them to one of its sessions. `row_position`: the live rows of one destination session take each of the positions from its resident length to its resident length plus their number minus 1 exactly once; 0 in slots that are not live. In every draw some session's rows end at position 1023. `resident_lengths`: A session's resident length plus its restored rows stays within 1024 positions. `key_cache`: entries of order one. `query`: entries of order one or a few tens.
All inputs are finite; a program needn't handle non-finite values.
Results may differ from a plain program's by a relative error of at most 0.009.
Values may be sent and summed in bfloat16 or wider, within the bound.
No kernel may reach another device: no remote copies, remote signals or barrier semaphores. Data moves between devices by JAX's collectives and lax.ppermute only.
A program may use at most 192 MiB of HBM per device.

v0:
```python
import math
import jax
import jax.numpy as jnp
from jax import lax
from jax.sharding import PartitionSpec as P

HDIM = 128
masked_score = -1e30


def local(
    hidden_rows,
    send_counts,
    row_session,
    row_position,
    resident_lengths,
    kv_weight,
    key_cache,
    value_cache,
    query,
    new_key,
    new_value,
):
    sources = hidden_rows.shape[1]
    slot_cap = hidden_rows.shape[2]
    slot_count = sources * slot_cap
    head_dev = query.shape[1] // HDIM
    sessions_dev = key_cache.shape[0]
    context = key_cache.shape[1]
    inverse_root = 1.0 / math.sqrt(HDIM)
    arrived, counts_in, session_in, position_in = (
        lax.all_to_all(hidden_rows, "inst", split_axis=1, concat_axis=0, tiled=True),
        lax.all_to_all(send_counts, "inst", split_axis=1, concat_axis=0, tiled=True),
        lax.all_to_all(row_session, "inst", split_axis=1, concat_axis=0, tiled=True),
        lax.all_to_all(row_position, "inst", split_axis=1, concat_axis=0, tiled=True),
    )
    full_rows = lax.all_gather(
        arrived.reshape(slot_count, arrived.shape[3]), "head", axis=1, tiled=True
    )
    restored = jnp.dot(
        full_rows,
        lax.all_gather(kv_weight, "inst", axis=0, tiled=True),
        preferred_element_type=jnp.float32,
    )
    restored = restored.astype(jnp.bfloat16).reshape(slot_count, head_dev, 2, HDIM)
    restored_keys = restored[:, :, 0]
    restored_values = restored[:, :, 1]
    slot_live = (jnp.arange(slot_cap)[None, :] < counts_in).reshape(slot_count)
    session_map = session_in.reshape(slot_count)
    position_map = position_in.reshape(slot_count)
    member = (session_map[None, :] == jnp.arange(sessions_dev)[:, None]) & slot_live[None, :]
    queries = query.reshape(sessions_dev, head_dev, HDIM)
    cache_keys = key_cache.reshape(sessions_dev, context, head_dev, HDIM)
    cache_values = value_cache.reshape(sessions_dev, context, head_dev, HDIM)
    own_score = (
        jnp.sum(
            queries.astype(jnp.float32)
            * new_key.reshape(sessions_dev, head_dev, HDIM).astype(jnp.float32),
            axis=-1,
        )
        * inverse_root
    )
    fresh_value = new_value.reshape(sessions_dev, head_dev, HDIM).astype(jnp.float32)
    position_ids = jnp.arange(context)
    target = jnp.where(slot_live, position_map, context)
    key_rows = cache_keys.at[session_map, target].set(restored_keys, mode="drop")
    value_rows = cache_values.at[session_map, target].set(restored_values, mode="drop")
    totals = resident_lengths + jnp.sum(member.astype(jnp.int32), axis=1)
    scores = (
        jnp.einsum("shd,sphd->shp", queries, key_rows, preferred_element_type=jnp.float32)
        * inverse_root
    )
    scores = jnp.where((position_ids[None, :] < totals[:, None])[:, None, :], scores, masked_score)
    highest = jnp.maximum(jnp.max(scores, axis=-1), own_score)
    weights = jnp.exp(scores - highest[:, :, None])
    own_weight = jnp.exp(own_score - highest)
    denominator = jnp.sum(weights, axis=-1) + own_weight
    probability = (weights / denominator[:, :, None]).astype(jnp.bfloat16)
    attended = jnp.einsum(
        "shp,sphd->shd", probability, value_rows, preferred_element_type=jnp.float32
    )
    own_prob = (own_weight / denominator).astype(jnp.bfloat16)
    attended = attended + own_prob.astype(jnp.float32)[:, :, None] * fresh_value
    return attended.astype(jnp.bfloat16).reshape(sessions_dev, head_dev * HDIM)


def solution(mesh):
    placed = (
        P("inst", None, None, "head"),
        P("inst", None),
        P("inst", None, None),
        P("inst", None, None),
        P("inst"),
        P("inst", "head"),
        P("inst", None, "head"),
        P("inst", None, "head"),
        P("inst", "head"),
        P("inst", "head"),
        P("inst", "head"),
    )
    return jax.shard_map(
        local, mesh=mesh, in_specs=placed, out_specs=P("inst", "head"), check_vma=False
    )
```

profile of v0, /device:TPU:1, one launch (start us, length us, event | category | flops | bytes accessed | tf_op | source)
XLA Modules:
  0.0 339.8 jit_solution(13822352009684851430)
XLA Ops:
  6.5 0.0 copy-start.4
  6.6 0.0 copy-start.1
  6.6 0.0 all-gather.3.cloned.1.call-start
  6.6 30.2 %all_to_all.40 = bf16[1,32,16,576]{3,2,0,1:T(8,128)(2,1)S(1)} all-to-all(bf16[1,32,16,576]{3,2,0,1:T(8,128)(2,1)} %bitcast.46), channel_id=1, replica_groups=mesh['inst'=32,'head'=16] {'inst'}, dimensions={1} | all-to-all | bytes 1179648 | tf_op jit(solution)/shard_map/all_to_all | solution.py:32
  36.9 1.1 copy.77
  37.9 0.0 all-gather.3.cloned.1.call-update
  37.9 0.0 all-gather.5.cloned.1.call-start
  38.0 0.7 all-gather.5.cloned.1.call-update
  38.7 0.0 copy-done.8
  38.7 0.7 copy.73
  39.4 8.4 %all-to-all-start.1 = ((s32[1,32,1]{2,0,1:T(1,128)}), s32[1,32,1]{2,0,1:T(1,128)S(1)}, u32[]{:S(2)}, u32[]{:S(2)}) async-start(s32[1,32,1]{2,0,1:T(1,128)} %copy.73), calls=%async_computation.1 | async-start | bytes 32768 | tf_op jit(solution)/shard_map/all_to_all | solution.py:33
  47.8 0.0 copy-done.5
  47.8 0.0 copy-done.6
  47.8 0.0 copy-done.3
  47.9 0.7 copy.72
  48.5 7.9 %all-to-all-done.1 = s32[1,32,1]{2,0,1:T(1,128)S(1)} async-done(((s32[1,32,1]{2,0,1:T(1,128)}), s32[1,32,1]{2,0,1:T(1,128)S(1)}, u32[]{:S(2)}, u32[]{:S(2)}) %all-to-all-start.1) | async-done | bytes 160 | tf_op jit(solution)/shard_map/all_to_all | solution.py:33
  56.4 3.8 %all-to-all-start = ((s32[1,32,16]{2,0,1:T(1,128)}), s32[1,32,16]{2,0,1:T(1,128)S(1)}, u32[]{:S(2)}, u32[]{:S(2)}) async-start(s32[1,32,16]{2,0,1:T(1,128)} %copy.72), calls=%async_computation | async-start | bytes 32768 | tf_op jit(solution)/shard_map/all_to_all | solution.py:34
  60.2 0.1 multiply_reduce_fusion
  60.3 0.1 copy.81
  60.4 0.0 copy-done.7
  60.4 0.0 copy-done.4
  60.4 0.7 copy.75
  61.1 0.0 copy-done.1
  61.1 0.7 copy.74
  61.9 0.0 copy-start.2
  61.9 2.6 copy.79
  64.5 0.0 copy-done.2
  64.5 0.7 copy.82
  65.3 0.0 copy-start.9
  65.3 2.6 copy.84
  67.9 0.7 reduce.1
  68.5 0.3 all-to-all-done
  68.8 9.1 %all-to-all-start.2 = ((s32[1,32,16]{2,0,1:T(1,128)}), s32[1,32,16]{2,0,1:T(1,128)S(1)}, u32[]{:S(2)}, u32[]{:S(2)}) async-start(s32[1,32,16]{2,0,1:T(1,128)} %copy.75), calls=%async_computation.2 | async-start | bytes 32768 | tf_op jit(solution)/shard_map/all_to_all | solution.py:35
  77.9 0.1 iota_compare_fusion
  78.0 0.1 lt.77
  78.1 0.1 lt.81
  78.2 0.1 reshape.176
  78.3 0.5 broadcast.131
  78.8 0.7 reduce.10
  79.5 0.1 eq.15
  79.6 6.8 %all-to-all-done.2 = s32[1,32,16]{2,0,1:T(1,128)S(1)} async-done(((s32[1,32,16]{2,0,1:T(1,128)}), s32[1,32,16]{2,0,1:T(1,128)S(1)}, u32[]{:S(2)}, u32[]{:S(2)}) %all-to-all-start.2) | async-done | bytes 2080 | tf_op jit(solution)/shard_map/all_to_all | solution.py:35
  86.4 0.7 reduce.9
  87.1 0.1 reshape.177
  87.2 0.1 fusion.8
  87.3 0.0 copy-done.9
  87.3 0.1 iota_compare_fusion.1
  87.4 15.0 %all-gather.3.cloned.1.call-done = bf16[512,9216]{0,1:T(8,128)(2,1)} async-done(((bf16[512,576]{0,1:T(8,128)(2,1)}), bf16[512,9216]{0,1:T(8,128)(2,1)}) %all-gather.3.cloned.1.call-update) | async-done | bytes 9437200 | tf_op jit(solution)/shard_map/all_gather | solution.py:37
  102.4 135.1 %all-gather.5.cloned.1.call-done = bf16[9216,768]{1,0:T(8,128)(2,1)} async-done(((bf16[288,768]{1,0:T(8,128)(2,1)}), bf16[9216,768]{1,0:T(8,128)(2,1)}) %all-gather.5.cloned.1.call-update) | async-done | bytes 14155792 | tf_op jit(solution)/shard_map/all_gather | solution.py:42
  237.4 14.2 %convolution_convert_fusion = bf16[512,768]{1,0:T(8,128)(2,1)S(1)} fusion(bf16[512,9216]{0,1:T(8,128)(2,1)} %all-gather.3.cloned.1.call-done, bf16[9216,768]{1,0:T(8,128)(2,1)} %all-gather.5.cloned.1.call-done), kind=kOutput, calls=%fused_computation.6 | convolution fusion | flops 7248150528 | bytes 24379392 | tf_op jit(solution)/shard_map/dot_general | solution.py:40
  251.6 0.2 reshape.179
  251.8 1.1 fusion.15
  252.9 0.1 copy_bitcast_fusion
  253.1 0.3 copy.85
  253.4 0.3 copy.80
  253.8 55.4 %scatter_fusion = bf16[2,1024,3,128]{3,2,1,0:T(4,128)(2,1)} fusion(bf16[2,1024,3,128]{3,2,1,0:T(4,128)(2,1)} %copy.79, s32[512]{0:T(512)S(1)} %bitcast.41, bf16[512,3,128]{2,1,0:T(4,128)(2,1)S(1)} %copy.80), kind=kCustom, calls=%fused_computation | custom fusion | bytes 1183744 | tf_op jit(solution)/shard_map/scatter | solution.py:66
  309.2 2.1 fusion.2
  311.3 0.1 fusion.14
  311.4 0.2 fusion.6
  311.6 0.1 fusion.7
  311.7 0.1 copy.86
  311.8 20.1 %scatter_fusion.1 = bf16[2,1024,3,128]{3,2,1,0:T(4,128)(2,1)S(1)} fusion(bf16[2,1024,3,128]{3,2,1,0:T(4,128)(2,1)S(1)} %copy-done, s32[512]{0:T(512)S(1)} %bitcast.42, bf16[512,3,128]{2,1,0:T(4,128)(2,1)S(1)} %copy.85), kind=kCustom, calls=%fused_computation.1 | custom fusion | bytes 1183744 | tf_op jit(solution)/shard_map/scatter | solution.py:67
  331.9 0.4 fusion
  332.3 0.1 fusion.11
  332.3 0.6 copy.115
  (15 shorter events, 0.1 us)
Async XLA Ops:
  6.5 32.2 %copy-start.8 = (s32[1,32]{1,0:T(1,128)S(1)}, s32[1,32]{1,0:T(1,128)}, u32[]{:S(2)}) copy-start(s32[1,32]{1,0:T(1,128)} %param.12) | copy-start | bytes 388
  6.5 41.3 %copy-start.5 = (bf16[2,384]{1,0:T(2,128)(2,1)S(1)}, bf16[2,384]{1,0:T(2,128)(2,1)}, u32[]{:S(2)}) copy-start(bf16[2,384]{1,0:T(2,128)(2,1)} %param.19) | copy-start | bytes 4612
  6.5 41.3 %copy-start.6 = (bf16[2,384]{1,0:T(2,128)(2,1)S(1)}, bf16[2,384]{1,0:T(2,128)(2,1)}, u32[]{:S(2)}) copy-start(bf16[2,384]{1,0:T(2,128)(2,1)} %param.20) | copy-start | bytes 4612
  6.5 41.3 %copy-start.3 = (s32[1,32,16]{1,2,0:T(8,128)S(1)}, s32[1,32,16]{1,2,0:T(8,128)}, u32[]{:S(2)}) copy-start(s32[1,32,16]{1,2,0:T(8,128)} %param.13) | copy-start | bytes 6148
  6.5 53.9 %copy-start.7 = (bf16[2,384]{1,0:T(2,128)(2,1)S(1)}, bf16[2,384]{1,0:T(2,128)(2,1)}, u32[]{:S(2)}) copy-start(bf16[2,384]{1,0:T(2,128)(2,1)} %param.21) | copy-start | bytes 4612
  6.5 53.9 %copy-start.4 = (s32[1,32,16]{1,2,0:T(8,128)S(1)}, s32[1,32,16]{1,2,0:T(8,128)}, u32[]{:S(2)}) copy-start(s32[1,32,16]{1,2,0:T(8,128)} %param.14) | copy-start | bytes 6148
  6.6 54.5 %copy-start.1 = (bf16[2,1024,384]{2,1,0:T(8,128)(2,1)S(1)}, bf16[2,1024,384]{2,1,0:T(8,128)(2,1)}, u32[]{:S(2)}) copy-start(bf16[2,1024,384]{2,1,0:T(8,128)(2,1)} %param.17) | copy-start | bytes 4718596
  6.6 95.8 %all-gather.3.cloned.1.call-start = ((), (), s32[]{:S(2)}) async-start(), calls=%async_computation.4 | async-start | bytes 10027008 | tf_op jit(solution)/shard_map/all_gather | solution.py:37
  37.9 199.5 %all-gather.5.cloned.1.call-start = ((), (), s32[]{:S(2)}) async-start(), calls=%async_computation.5 | async-start | bytes 14598144 | tf_op jit(solution)/shard_map/all_gather | solution.py:42
  39.4 17.0 %all-to-all-start.1 = ((s32[1,32,1]{2,0,1:T(1,128)}), s32[1,32,1]{2,0,1:T(1,128)S(1)}, u32[]{:S(2)}, u32[]{:S(2)}) async-start(s32[1,32,1]{2,0,1:T(1,128)} %copy.73), calls=%async_computation.1 | async-start | bytes 32768 | tf_op jit(solution)/shard_map/all_to_all | solution.py:33
  56.4 12.4 %all-to-all-start = ((s32[1,32,16]{2,0,1:T(1,128)}), s32[1,32,16]{2,0,1:T(1,128)S(1)}, u32[]{:S(2)}, u32[]{:S(2)}) async-start(s32[1,32,16]{2,0,1:T(1,128)} %copy.72), calls=%async_computation | async-start | bytes 32768 | tf_op jit(solution)/shard_map/all_to_all | solution.py:34
  61.9 2.6 copy-start.2
  65.3 22.0 %copy-start.9 = (s32[2]{0:T(128)S(1)}, s32[2]{0:T(128)}, u32[]{:S(2)}) copy-start(s32[2]{0:T(128)} %param.15) | copy-start | bytes 28
  68.8 17.6 %all-to-all-start.2 = ((s32[1,32,16]{2,0,1:T(1,128)}), s32[1,32,16]{2,0,1:T(1,128)S(1)}, u32[]{:S(2)}, u32[]{:S(2)}) async-start(s32[1,32,16]{2,0,1:T(1,128)} %copy.75), calls=%async_computation.2 | async-start | bytes 32768 | tf_op jit(solution)/shard_map/all_to_all | solution.py:35
  253.8 58.1 %copy-start = (bf16[2,1024,3,128]{3,2,1,0:T(4,128)(2,1)S(1)}, bf16[2,1024,3,128]{3,2,1,0:T(4,128)(2,1)}, u32[]{:S(2)}) copy-start(bf16[2,1024,3,128]{3,2,1,0:T(4,128)(2,1)} %copy.84) | copy-start | bytes 4718596
Sparse Core Ops, SparseCore 0:
  38.1 64.2 all-gather.2
  105.5 131.8 all-gather.4
where the time goes:
time: 341 us; the launch traced here: 340 us
  waiting for transfers between devices  166 us (49%)
  local copies, waits for them, and re-layouts  89.2 us (26%)
  blocking collectives  30.2 us (9%)
  starting transfers between devices  21.4 us (6%)
  matrix products  16.6 us (5%)
  between operations  13.6 us (4%)
    all_gather x1, waiting for transfers between devices, local(): lax.all_gather(kv_weight, 'inst', axis=0, tiled=True)  135 us
    scatter x1, local copies, waits for them, and re-layouts, local(): cache_keys.at[session_map, target].set(restored_keys, mode='drop')  55.4 us
    all_to_all x1, blocking collectives, local(): lax.all_to_all(hidden_rows, 'inst', split_axis=1, concat_axis=0, tiled=True)  30.2 us
    scatter x1, local copies, waits for them, and re-layouts, local(): cache_values.at[session_map, target].set(restored_values, mode='drop')  20.1 us
    all_gather x1, waiting for transfers between devices, local(): lax.all_gather(arrived.reshape(slot_count, arrived.shape[3]), 'head', axi...  15 us
    dot_general x1, matrix products, local(): jnp.dot(full_rows, lax.all_gather(kv_weight, 'inst', axis=0, tiled=True),...  14.2 us
    all_to_all x1, starting transfers between devices, local(): lax.all_to_all(row_position, 'inst', split_axis=1, concat_axis=0, tiled=T...  9.1 us
    all_to_all x1, starting transfers between devices, local(): lax.all_to_all(send_counts, 'inst', split_axis=1, concat_axis=0, tiled=True)  8.39 us
  transfers between devices with their start and end apart: 5, of which 5 were waited for; matrix products, arithmetic and copies ran while one was open for 4% of the time, Pallas kernels for 0%

commit v1 on v0

--- a/solution.py
+++ b/solution.py
@@ -32,7 +32,12 @@
         lax.all_to_all(hidden_rows, "inst", split_axis=1, concat_axis=0, tiled=True),
         lax.all_to_all(send_counts, "inst", split_axis=1, concat_axis=0, tiled=True),
         lax.all_to_all(row_session, "inst", split_axis=1, concat_axis=0, tiled=True),
-        lax.all_to_all(row_position, "inst", split_axis=1, concat_axis=0, tiled=True),
+        jnp.concatenate(
+            lax.all_to_all(
+                jnp.stack(jnp.split(row_position, lax.axis_size("inst"), axis=1)), "inst", 0, 0
+            ),
+            axis=0,
+        ),
     )
     full_rows = lax.all_gather(
         arrived.reshape(slot_count, arrived.shape[3]), "head", axis=1, tiled=True

time: 341 us -> 341 us (level)
  waiting for transfers between devices: 166 us -> 143 us
  local copies, waits for them, and re-layouts: 89.2 us -> 107 us
  starting transfers between devices: 21.4 us -> 26.8 us
    unnamed x25 -> x55, local copies, waits for them, and re-layouts: 3.47 us -> 19.7 us
    all_gather x1, waiting for transfers between devices: 15 us -> 0.02 us  [local(): lax.all_gather(arrived.reshape(slot_count, arrived.shape[3]), 'head', axi...]
    all_to_all x1, waiting for transfers between devices: 7.89 us -> 0.01 us  [local(): lax.all_to_all(send_counts, 'inst', split_axis=1, concat_axis=0, tiled=True)]
    all_to_all x1, waiting for transfers between devices: 0.32 us -> 6.91 us  [local(): lax.all_to_all(row_session, 'inst', split_axis=1, concat_axis=0, tiled=True)]
    all_to_all x1, waiting for transfers between devices: 6.81 us -> 0.3 us  [local(): lax.all_to_all(jnp.stack(jnp.split(row_position, lax.axis_size('inst'), a...]
    all_to_all x1, starting transfers between devices: 3.78 us -> 9.13 us  [local(): lax.all_to_all(row_session, 'inst', split_axis=1, concat_axis=0, tiled=True)]
  transfers between devices with their start and end apart: 5 -> 5, of which waited for: 5 -> 3; matrix products, arithmetic and copies ran while one was open for 4% -> 9% of each run, Pallas kernels for 0% -> 0%
where the time goes in v1:
time: 341 us; the launch traced here: 339 us
  waiting for transfers between devices  143 us (42%)
  local copies, waits for them, and re-layouts  107 us (31%)
  blocking collectives  30.2 us (9%)
  starting transfers between devices  26.8 us (8%)
  matrix products  16.6 us (5%)
  between operations  13.6 us (4%)
    all_gather x1, waiting for transfers between devices, local(): lax.all_gather(kv_weight, 'inst', axis=0, tiled=True)  135 us
    scatter x1, local copies, waits for them, and re-layouts, local(): cache_keys.at[session_map, target].set(restored_keys, mode='drop')  55.1 us
    all_to_all x1, blocking collectives, local(): lax.all_to_all(hidden_rows, 'inst', split_axis=1, concat_axis=0, tiled=True)  30.2 us
    scatter x1, local copies, waits for them, and re-layouts, local(): cache_values.at[session_map, target].set(restored_values, mode='drop')  20.1 us
    unnamed x55, local copies, waits for them, and re-layouts  19.7 us
    dot_general x1, matrix products, local(): jnp.dot(full_rows, lax.all_gather(kv_weight, 'inst', axis=0, tiled=True),...  14.2 us
    all_to_all x1, starting transfers between devices, local(): lax.all_to_all(jnp.stack(jnp.split(row_position, lax.axis_size('inst'), a...  9.24 us
    all_to_all x1, starting transfers between devices, local(): lax.all_to_all(row_session, 'inst', split_axis=1, concat_axis=0, tiled=True)  9.13 us
  transfers between devices with their start and end apart: 5, of which 3 were waited for; matrix products, arithmetic and copies ran while one was open for 9% of the time, Pallas kernels for 0%

profile of v1, /device:TPU:1, one launch (start us, length us, event | category | flops | bytes accessed | tf_op | source)
XLA Modules:
  0.0 339.5 jit_solution(10518289951586894548)
XLA Ops:
  6.6 30.2 %all_to_all.36 = bf16[1,32,16,576]{3,2,0,1:T(8,128)(2,1)S(1)} all-to-all(bf16[1,32,16,576]{3,2,0,1:T(8,128)(2,1)} %bitcast.109), channel_id=1, replica_groups=mesh['inst'=32,'head'=16] {'inst'}, dimensions={1} | all-to-all | bytes 1179648 | tf_op jit(solution)/shard_map/all_to_all | solution.py:32
  36.9 1.1 copy.71
  38.0 0.7 all-gather.5.cloned.1.call-update
  38.7 0.7 copy.68
  39.4 8.4 %all-to-all-start.1 = ((s32[1,32,1]{2,0,1:T(1,128)}), s32[1,32,1]{2,0,1:T(1,128)S(1)}, u32[]{:S(2)}, u32[]{:S(2)}) async-start(s32[1,32,1]{2,0,1:T(1,128)} %copy.68), calls=%async_computation.1 | async-start | bytes 32768 | tf_op jit(solution)/shard_map/all_to_all | solution.py:33
  47.8 0.4 slice_reduce_fusion.1
  48.2 0.5 slice_reduce_fusion
  48.8 0.5 constant_dynamic-update-slice_fusion.31
  49.3 0.5 constant_dynamic-update-slice_fusion.30
  49.8 0.5 constant_dynamic-update-slice_fusion.29
  50.3 0.5 constant_dynamic-update-slice_fusion.28
  50.9 0.5 constant_dynamic-update-slice_fusion.27
  51.4 0.6 constant_dynamic-update-slice_fusion.26
  51.9 0.5 constant_dynamic-update-slice_fusion.25
  52.5 0.6 constant_dynamic-update-slice_fusion.24
  53.1 0.5 constant_dynamic-update-slice_fusion.23
  53.6 0.5 constant_dynamic-update-slice_fusion.22
  54.1 0.5 constant_dynamic-update-slice_fusion.21
  54.6 0.5 constant_dynamic-update-slice_fusion.20
  55.2 0.5 constant_dynamic-update-slice_fusion.19
  55.7 0.6 constant_dynamic-update-slice_fusion.18
  56.3 0.5 constant_dynamic-update-slice_fusion.17
  56.8 0.6 constant_dynamic-update-slice_fusion.16
  57.4 0.6 constant_dynamic-update-slice_fusion.15
  58.0 0.6 constant_dynamic-update-slice_fusion.14
  58.5 0.6 constant_dynamic-update-slice_fusion.13
  59.1 0.6 constant_dynamic-update-slice_fusion.12
  59.7 0.5 constant_dynamic-update-slice_fusion.11
  60.2 0.5 constant_dynamic-update-slice_fusion.10
  60.7 0.5 constant_dynamic-update-slice_fusion.9
  61.2 0.5 constant_dynamic-update-slice_fusion.8
  61.8 0.6 constant_dynamic-update-slice_fusion.7
  62.4 0.6 constant_dynamic-update-slice_fusion.6
  62.9 0.6 constant_dynamic-update-slice_fusion.5
  63.5 0.6 constant_dynamic-update-slice_fusion.4
  64.1 0.5 constant_dynamic-update-slice_fusion.3
  64.6 0.6 constant_dynamic-update-slice_fusion.2
  65.2 0.5 constant_dynamic-update-slice_fusion.1
  65.7 0.5 constant_dynamic-update-slice_fusion
  66.2 9.2 %all-to-all-start.2 = ((s32[32,1,1,16]{3,2,1,0:T(1,128)}), s32[32,1,1,16]{3,2,1,0:T(1,128)S(1)}, u32[]{:S(2)}, u32[]{:S(2)}) async-start(s32[32,1,1,16]{3,2,1,0:T(1,128)} %constant_dynamic-update-slice_fusion), calls=%async_computation.2 | async-start | bytes 32768 | tf_op jit(solution)/shard_map/all_to_all | solution.py:36
  75.7 0.7 copy.67
  76.4 0.7 copy.69
  77.1 2.6 copy.73
  79.8 0.7 copy.76
  80.6 2.6 copy.78
  83.2 0.7 reduce.1
  83.8 0.3 all-to-all-done.2
  84.1 9.1 %all-to-all-start = ((s32[1,32,16]{2,0,1:T(1,128)}), s32[1,32,16]{2,0,1:T(1,128)S(1)}, u32[]{:S(2)}, u32[]{:S(2)}) async-start(s32[1,32,16]{2,0,1:T(1,128)} %copy.67), calls=%async_computation | async-start | bytes 32768 | tf_op jit(solution)/shard_map/all_to_all | solution.py:34
  93.5 0.5 broadcast.163
  94.0 0.7 reduce.73
  94.8 6.9 %all-to-all-done = s32[1,32,16]{2,0,1:T(1,128)S(1)} async-done(((s32[1,32,16]{2,0,1:T(1,128)}), s32[1,32,16]{2,0,1:T(1,128)S(1)}, u32[]{:S(2)}, u32[]{:S(2)}) %all-to-all-start) | async-done | bytes 2080 | tf_op jit(solution)/shard_map/all_to_all | solution.py:34
  101.8 0.7 reduce.74
  102.8 134.6 %all-gather.5.cloned.1.call-done = bf16[9216,768]{1,0:T(8,128)(2,1)} async-done(((bf16[288,768]{1,0:T(8,128)(2,1)}), bf16[9216,768]{1,0:T(8,128)(2,1)}) %all-gather.5.cloned.1.call-update) | async-done | bytes 14155792 | tf_op jit(solution)/shard_map/all_gather | solution.py:47
  237.5 14.2 %convolution_convert_fusion = bf16[512,768]{1,0:T(8,128)(2,1)S(1)} fusion(bf16[512,9216]{0,1:T(8,128)(2,1)} %all-gather.3.cloned.1.call-done, bf16[9216,768]{1,0:T(8,128)(2,1)} %all-gather.5.cloned.1.call-done), kind=kOutput, calls=%fused_computation.6 | convolution fusion | flops 7248150528 | bytes 24379392 | tf_op jit(solution)/shard_map/dot_general | solution.py:45
  251.6 0.2 reshape.171
  251.8 1.1 fusion.15
  253.1 0.3 copy.79
  253.4 0.3 copy.74
  253.8 55.1 %scatter_fusion = bf16[2,1024,3,128]{3,2,1,0:T(4,128)(2,1)} fusion(bf16[2,1024,3,128]{3,2,1,0:T(4,128)(2,1)} %copy.73, s32[512]{0:T(512)S(1)} %bitcast.104, bf16[512,3,128]{2,1,0:T(4,128)(2,1)S(1)} %copy.74), kind=kCustom, calls=%fused_computation | custom fusion | bytes 1183744 | tf_op jit(solution)/shard_map/scatter | solution.py:71
  308.9 2.1 fusion.2
  311.1 0.2 fusion.6
  311.5 20.1 %scatter_fusion.1 = bf16[2,1024,3,128]{3,2,1,0:T(4,128)(2,1)S(1)} fusion(bf16[2,1024,3,128]{3,2,1,0:T(4,128)(2,1)S(1)} %copy-done.1, s32[512]{0:T(512)S(1)} %bitcast.105, bf16[512,3,128]{2,1,0:T(4,128)(2,1)S(1)} %copy.79), kind=kCustom, calls=%fused_computation.1 | custom fusion | bytes 1183744 | tf_op jit(solution)/shard_map/scatter | solution.py:72
  331.6 0.4 fusion
  332.1 0.6 copy.109
  (48 shorter events, 1.7 us)
Async XLA Ops:
  6.5 32.2 %copy-start.8 = (s32[1,32]{1,0:T(1,128)S(1)}, s32[1,32]{1,0:T(1,128)}, u32[]{:S(2)}) copy-start(s32[1,32]{1,0:T(1,128)} %param.12) | copy-start | bytes 388
  6.5 41.3 %copy-start = (s32[1,32,16]{1,2,0:T(8,128)S(1)}, s32[1,32,16]{1,2,0:T(8,128)}, u32[]{:S(2)}) copy-start(s32[1,32,16]{1,2,0:T(8,128)} %param.14) | copy-start | bytes 6148
  6.5 59.6 %copy-start.5 = (bf16[2,384]{1,0:T(2,128)(2,1)S(1)}, bf16[2,384]{1,0:T(2,128)(2,1)}, u32[]{:S(2)}) copy-start(bf16[2,384]{1,0:T(2,128)(2,1)} %param.19) | copy-start | bytes 4612
  6.5 59.7 %copy-start.6 = (bf16[2,384]{1,0:T(2,128)(2,1)S(1)}, bf16[2,384]{1,0:T(2,128)(2,1)}, u32[]{:S(2)}) copy-start(bf16[2,384]{1,0:T(2,128)(2,1)} %param.20) | copy-start | bytes 4612
  6.5 69.1 %copy-start.7 = (bf16[2,384]{1,0:T(2,128)(2,1)S(1)}, bf16[2,384]{1,0:T(2,128)(2,1)}, u32[]{:S(2)}) copy-start(bf16[2,384]{1,0:T(2,128)(2,1)} %param.21) | copy-start | bytes 4612
  6.5 69.1 %copy-start.4 = (s32[1,32,16]{1,2,0:T(8,128)S(1)}, s32[1,32,16]{1,2,0:T(8,128)}, u32[]{:S(2)}) copy-start(s32[1,32,16]{1,2,0:T(8,128)} %param.13) | copy-start | bytes 6148
  6.6 69.8 %copy-start.2 = (bf16[2,1024,384]{2,1,0:T(8,128)(2,1)S(1)}, bf16[2,1024,384]{2,1,0:T(8,128)(2,1)}, u32[]{:S(2)}) copy-start(bf16[2,1024,384]{2,1,0:T(8,128)(2,1)} %param.17) | copy-start | bytes 4718596
  6.6 96.2 %all-gather.3.cloned.1.call-start = ((), (), s32[]{:S(2)}) async-start(), calls=%async_computation.4 | async-start | bytes 10027008 | tf_op jit(solution)/shard_map/all_gather | solution.py:42
  38.0 199.5 %all-gather.5.cloned.1.call-start = ((), (), s32[]{:S(2)}) async-start(), calls=%async_computation.5 | async-start | bytes 14598144 | tf_op jit(solution)/shard_map/all_gather | solution.py:47
  39.4 26.8 %all-to-all-start.1 = ((s32[1,32,1]{2,0,1:T(1,128)}), s32[1,32,1]{2,0,1:T(1,128)S(1)}, u32[]{:S(2)}, u32[]{:S(2)}) async-start(s32[1,32,1]{2,0,1:T(1,128)} %copy.68), calls=%async_computation.1 | async-start | bytes 32768 | tf_op jit(solution)/shard_map/all_to_all | solution.py:33
  66.2 17.9 %all-to-all-start.2 = ((s32[32,1,1,16]{3,2,1,0:T(1,128)}), s32[32,1,1,16]{3,2,1,0:T(1,128)S(1)}, u32[]{:S(2)}, u32[]{:S(2)}) async-start(s32[32,1,1,16]{3,2,1,0:T(1,128)} %constant_dynamic-update-slice_fusion), calls=%async_computation.2 | async-start | bytes 32768 | tf_op jit(solution)/shard_map/all_to_all | solution.py:36
  77.1 2.6 copy-start.3
  80.5 22.1 %copy-start.9 = (s32[2]{0:T(128)S(1)}, s32[2]{0:T(128)}, u32[]{:S(2)}) copy-start(s32[2]{0:T(128)} %param.15) | copy-start | bytes 28
  84.1 17.6 %all-to-all-start = ((s32[1,32,16]{2,0,1:T(1,128)}), s32[1,32,16]{2,0,1:T(1,128)S(1)}, u32[]{:S(2)}, u32[]{:S(2)}) async-start(s32[1,32,16]{2,0,1:T(1,128)} %copy.67), calls=%async_computation | async-start | bytes 32768 | tf_op jit(solution)/shard_map/all_to_all | solution.py:34
  253.8 57.8 %copy-start.1 = (bf16[2,1024,3,128]{3,2,1,0:T(4,128)(2,1)S(1)}, bf16[2,1024,3,128]{3,2,1,0:T(4,128)(2,1)}, u32[]{:S(2)}) copy-start(bf16[2,1024,3,128]{3,2,1,0:T(4,128)(2,1)} %copy.78) | copy-start | bytes 4718596
Sparse Core Ops, SparseCore 0:
  38.1 64.2 all-gather.2
  105.5 131.8 all-gather.4
